TPU v7x, 512 devices: a whole 4x4x16 slice. The times are simulated.
512 devices in a mesh: tensor: 16 (over x, z_hi), feature: 8 (over y, core), dp: 4 (over z_lo).
Axes of the slice: x: 4, y: 4, z: 16 (z_hi: 4, z_lo: 4; z = z_hi * 4 + z_lo), core: 2. Of those that a mesh axis runs over, the one named last changes fastest.
Arguments:
- mlp_input: bfloat16 [64, 4096], P(None, ('feature', 'dp')), may hold values from -6 to 6
- gate_weight: bfloat16 [4096, 28672], P(('feature', 'dp'), 'tensor'), may hold values from -0.09375 to 0.09375
- up_weight: bfloat16 [4096, 28672], P(('feature', 'dp'), 'tensor'), may hold values from -0.09375 to 0.09375
- down_weight: bfloat16 [28672, 4096], P('tensor', ('feature', 'dp')), may hold values from -0.03125 to 0.03125
- down_encoder: bfloat16 [65536, 4096], P('tensor', ('feature', 'dp')), may hold values from -6 to 6
- feature_ids: int32 [32], replicated, may hold values from 0 to 65535
- up_decoder: bfloat16 [131072, 4096], P('tensor', ('feature', 'dp')), may hold values from -0.09375 to 0.09375
- latent_ids: int32 [64, 64], replicated, may hold values from 0 to 131071, as said below
- latent_acts: float32 [64, 64], P('dp', 'tensor'), may hold values from 0.5 to 4
Outputs:
- attribution: float32 [32, 64, 64], P('feature', 'dp', 'tensor')
Inputs may be any that keep to these rules, and one draw needn't show every extreme that they name: `latent_ids`: the 64 latents of one token are distinct.
All inputs are finite; a program needn't handle non-finite values.
Results may differ from a plain program's by a relative error of at most 0.0029.
Values may be sent and summed in bfloat16 or wider, within the bound.
No kernel may reach another device: no remote copies, remote signals or barrier semaphores. Data moves between devices by JAX's collectives and lax.ppermute only.
A program may use at most 64 MiB of HBM per device.

v0:
```python
import math
import jax
import jax.numpy as jnp
from jax import lax
from jax.sharding import PartitionSpec as P


def factors(gate_pre, up_pre):
    sigmoid_gate = jax.nn.sigmoid(gate_pre)
    gate_factor = up_pre * sigmoid_gate * (1.0 + gate_pre * (1.0 - sigmoid_gate))
    up_factor = gate_pre * sigmoid_gate
    return (gate_factor, up_factor)


def arrange_blocks(partial_value, count_tensor, count_feature, count_data):
    features = partial_value.shape[0]
    tokens = partial_value.shape[1]
    slots = partial_value.shape[2]
    arranged = partial_value.reshape(
        count_feature,
        features // count_feature,
        count_data,
        tokens // count_data,
        count_tensor,
        slots // count_tensor,
    )
    arranged = arranged.transpose(4, 0, 2, 1, 3, 5)
    return arranged.reshape(
        count_tensor * count_feature * count_data,
        features // count_feature,
        tokens // count_data,
        slots // count_tensor,
    )


def on_device(
    mlp_input,
    gate_weight,
    up_weight,
    down_weight,
    down_encoder,
    feature_ids,
    up_decoder,
    latent_ids,
    latent_acts,
):
    contract = (((1,), (1,)), ((), ()))
    tensor_rank = lax.axis_index("tensor")
    tokens = mlp_input.shape[0]
    dblk = gate_weight.shape[0]
    ffblk = gate_weight.shape[1]
    features = feature_ids.shape[0]
    count_tensor = lax.axis_size("tensor")
    count_feature = lax.axis_size("feature")
    count_data = lax.axis_size("dp")
    enc_rows = down_encoder.shape[0]
    local_ids = feature_ids - tensor_rank * enc_rows
    picker = (local_ids[:, None] == jnp.arange(enc_rows, dtype=jnp.int32)[None, :]).astype(
        jnp.bfloat16
    )
    chosen = lax.psum(jnp.dot(picker, down_encoder, preferred_element_type=jnp.float32), "tensor")
    cotangent = chosen.astype(jnp.bfloat16)
    neuron_part = lax.dot_general(
        cotangent, down_weight, contract, preferred_element_type=jnp.float32
    )
    gate_part = jnp.dot(mlp_input, gate_weight, preferred_element_type=jnp.float32)
    up_part = jnp.dot(mlp_input, up_weight, preferred_element_type=jnp.float32)
    gate_pre, up_pre, neuron_grad = lax.psum((gate_part, up_part, neuron_part), ("feature", "dp"))
    gate_factor, up_factor = factors(gate_pre, up_pre)
    per_block = math.gcd(features, 8)
    grouped_rows = neuron_grad.reshape(features // per_block, per_block, ffblk)

    def feature_block(grad_rows):
        grad_gate = (
            (grad_rows[:, None, :] * gate_factor[None])
            .astype(jnp.bfloat16)
            .reshape(per_block * tokens, ffblk)
        )
        grad_up = (
            (grad_rows[:, None, :] * up_factor[None])
            .astype(jnp.bfloat16)
            .reshape(per_block * tokens, ffblk)
        )
        width_grad = lax.dot_general(
            grad_gate, gate_weight, contract, preferred_element_type=jnp.float32
        )
        width_grad = width_grad + lax.dot_general(
            grad_up, up_weight, contract, preferred_element_type=jnp.float32
        )
        return width_grad.reshape(per_block, tokens, dblk)

    width_part = lax.map(feature_block, grouped_rows).reshape(features, tokens, dblk)
    dec_rows = up_decoder.shape[0]
    local_latents = latent_ids - tensor_rank * dec_rows
    owner_mask = jnp.logical_and(local_latents >= 0, local_latents < dec_rows)
    picked = jnp.take(up_decoder, jnp.clip(local_latents, 0, dec_rows - 1), axis=0)
    picked = picked * owner_mask[:, :, None].astype(jnp.bfloat16)
    width_full = lax.psum(width_part, "tensor")
    partial_value = jnp.einsum(
        "ftd,tkd->ftk", width_full, picked.astype(jnp.float32), precision=lax.Precision.HIGHEST
    )
    arranged = arrange_blocks(partial_value, count_tensor, count_feature, count_data)
    own_block = lax.psum_scatter(
        arranged, ("tensor", "feature", "dp"), scatter_dimension=0, tiled=True
    )[0]
    return own_block * latent_acts[None, :, :]


def solution(mesh):
    in_specs = (
        P(None, ("feature", "dp")),
        P(("feature", "dp"), "tensor"),
        P(("feature", "dp"), "tensor"),
        P("tensor", ("feature", "dp")),
        P("tensor", ("feature", "dp")),
        P(),
        P("tensor", ("feature", "dp")),
        P(),
        P("dp", "tensor"),
    )
    out_specs = P("feature", "dp", "tensor")
    return jax.shard_map(
        on_device, mesh=mesh, in_specs=in_specs, out_specs=out_specs, check_vma=False
    )
```

profile of v0, /device:TPU:2, one launch (start us, length us, event | category | flops | bytes accessed | tf_op | source)
XLA Modules:
  0.0 1137.1 jit_solution(10292003025647488974)
XLA Ops:
  6.6 0.8 broadcast_subtract_fusion
  7.4 1.6 fusion.5
  9.0 99.8 %psum.35 = bf16[32,128]{1,0:T(8,128)(2,1)S(1)} all-reduce(f32[32,128]{1,0:T(8,128)S(1)} %fusion.5), channel_id=1, replica_groups=mesh['tensor'=16,'feature'=8,'dp'=4] {'tensor'}, use_global_device_ids=true, to_apply=%region_0.0 | all-reduce | flops 4096 | bytes 24576 | tf_op jit(solution)/shard_map/psum | solution.py:61
  108.8 2.0 fusion.12
  110.8 1.7 fusion.13
  112.5 1.0 convolution_bitcast_fusion
  113.5 283.3 %all-reduce.10.cloned.1.call-done = (f32[4,8,1792]{2,1,0:T(8,128)}, f32[64,1792]{1,0:T(8,128)}, f32[64,1792]{1,0:T(8,128)}) async-done(((f32[4,8,1792]{2,1,0:T(8,128)}, f32[64,1792]{1,0:T(8,128)}, f32[64,1792]{1,0:T(8,128)}), (f32[4,8,1792]{2,1,0:T(8,128)}, f32[64,1792]{1,0:T(8,128)}, f32[64,1792]{1,0:T(8,128)})) %all-reduce.10.cloned.1.call-update) | async-done | bytes 1146896 | tf_op jit(solution)/shard_map/psum | solution.py:68
  396.9 1.4 fusion.6
  398.2 16.5 %while.10 = (s32[]{:T(128)}, f32[4,8,64,128]{3,1,0,2:T(8,128)}, f32[4,8,1792]{2,1,0:T(8,128)}, f32[64,1792]{1,0:T(8,128)S(1)}, bf16[128,1792]{1,0:T(8,128)(2,1)S...) while((s32[]{:T(128)}, f32[4,8,64,128]{3,1,0,2:T(8,128)}, f32[4,8,1792]{2,1,0:T(8,128)}, ...), condition=%wide.region_5.6_spmd, body=%wide.region_4.5_spmd.sunk | while | flops 473497600 | bytes 12493429 | solution.py:92
  398.3 0.8 dynamic-slice_bitcast_fusion.3
  399.1 0.7 multiply_convert_fusion.3
  401.5 0.9 copy_dynamic-update-slice_fusion.2
  402.4 0.8 dynamic-slice_bitcast_fusion.3
  403.2 0.7 multiply_convert_fusion.3
  404.9 0.6 convolution_add_fusion.2
  405.6 0.9 copy_dynamic-update-slice_fusion.2
  406.5 0.8 dynamic-slice_bitcast_fusion.3
  407.3 0.7 multiply_convert_fusion.3
  409.0 0.6 convolution_add_fusion.2
  409.7 0.9 copy_dynamic-update-slice_fusion.2
  410.6 0.8 dynamic-slice_bitcast_fusion.3
  411.5 0.7 multiply_convert_fusion.3
  413.9 0.9 copy_dynamic-update-slice_fusion.2
  415.0 12.1 %gather_fusion = bf16[4096,128]{1,0:T(8,128)(2,1)S(1)} fusion(bf16[8192,128]{1,0:T(8,128)(2,1)S(1)} %copy-done, s32[4096]{0:T(1024)S(1)} %broadcast_clamp_fusion), kind=kCustom, calls=%fused_computation | custom fusion | bytes 2113536 | tf_op jit(solution)/shard_map/jit(_take)/gather | solution.py:96
  427.1 197.9 %all-reduce.6.cloned.1.call-done = f32[32,64,128]{2,0,1:T(8,128)} async-done(((f32[32,64,128]{2,0,1:T(8,128)}), f32[32,64,128]{2,0,1:T(8,128)}) %all-reduce.6.cloned.1.call-update) | async-done | bytes 1048592 | tf_op jit(solution)/shard_map/psum | solution.py:98
  625.0 4.4 convolution_bitcast_fusion.1
  629.3 1.8 copy.18
  631.1 3.2 reshape.39
  634.3 3.4 copy.19
  637.7 4.7 copy.20
  642.4 486.8 %all-reduce.8.cloned.1.call-done = f32[512,4,16,4]{2,3,1,0:T(4,128)} async-done(((f32[512,4,16,4]{2,3,1,0:T(4,128)}), f32[512,4,16,4]{2,3,1,0:T(4,128)}) %all-reduce.8.cloned.1.call-update) | async-done | bytes 524304
  1129.2 1.3 fusion.8
  (34 shorter events, 5.6 us)
Async XLA Ops:
  6.5 408.4 %copy-start = (bf16[8192,128]{1,0:T(8,128)(2,1)S(1)}, bf16[8192,128]{1,0:T(8,128)(2,1)}, u32[]{:S(2)}) copy-start(bf16[8192,128]{1,0:T(8,128)(2,1)} %param.17) | copy-start | bytes 6291460
  6.5 104.3 %copy-start.1 = (bf16[128,1792]{1,0:T(8,128)(2,1)S(1)}, bf16[128,1792]{1,0:T(8,128)(2,1)}, u32[]{:S(2)}) copy-start(bf16[128,1792]{1,0:T(8,128)(2,1)} %param.12) | copy-start | bytes 1376260
  6.5 106.0 %copy-start.3 = (bf16[1792,128]{1,0:T(8,128)(2,1)S(1)}, bf16[1792,128]{1,0:T(8,128)(2,1)}, u32[]{:S(2)}) copy-start(bf16[1792,128]{1,0:T(8,128)(2,1)} %param.14) | copy-start | bytes 1376260
  6.5 390.3 %all-reduce.10.cloned.1.call-start = ((), (), s32[]{:S(2)}) async-start(), calls=%async_computation.2 | async-start | bytes 2293760 | tf_op jit(solution)/shard_map/psum | solution.py:68
  113.5 511.5 %all-reduce.6.cloned.1.call-start = ((), (), s32[]{:S(2)}) async-start(), calls=%async_computation | async-start | bytes 2097152 | tf_op jit(solution)/shard_map/psum | solution.py:98
  398.2 16.6 %copy-start.4 = (s32[64,64]{1,0:T(8,128)S(1)}, s32[64,64]{1,0:T(8,128)}, u32[]{:S(2)}) copy-start(s32[64,64]{1,0:T(8,128)} %param.18) | copy-start | bytes 49156
  399.8 1.0 copy-start.2
  403.9 1.0 copy-start.2
  408.0 1.0 copy-start.2
  412.2 1.0 copy-start.2
  414.8 714.4 %all-reduce.8.cloned.1.call-start = ((), (), s32[]{:S(2)}) async-start(), calls=%async_computation.1 | async-start | bytes 8388608
  642.4 486.9 %copy-start.5 = (f32[16,4]{0,1:T(4,128)S(1)}, f32[16,4]{0,1:T(4,128)}, u32[]{:S(2)}) copy-start(f32[16,4]{0,1:T(4,128)} %param.19) | copy-start | bytes 772
Sparse Core Ops, SparseCore 0:
  113.6 283.2 all-reduce.9
  414.9 210.0 all-reduce.5
  642.5 486.6 all-reduce.7
where the time goes:
time: 1140 us
  waiting for transfers between devices  968 us (85%)
  blocking collectives  99.8 us (9%)
  local copies, waits for them, and re-layouts  33.6 us (3%)
  matrix products  15.8 us (1%)
  between operations  13.2 us (1%)
    unnamed x4, waiting for transfers between devices  487 us
    psum x1, waiting for transfers between devices, on_device(): lax.psum((gate_part, up_part, neuron_part), ('feature', 'dp'))  283 us
    psum x1, waiting for transfers between devices, on_device(): width_full = lax.psum(width_part, 'tensor')  198 us
    psum x1, blocking collectives, on_device(): lax.psum(jnp.dot(picker, down_encoder, preferred_element_type=jnp.float32...  99.8 us
  transfers between devices with their start and end apart: 3, of which 3 were waited for; matrix products, arithmetic and copies ran while one was open for 1% of the time, Pallas kernels for 0%

commit v1 on v0

--- a/solution.py
+++ b/solution.py
@@ -65,7 +65,10 @@
     )
     gate_part = jnp.dot(mlp_input, gate_weight, preferred_element_type=jnp.float32)
     up_part = jnp.dot(mlp_input, up_weight, preferred_element_type=jnp.float32)
-    gate_pre, up_pre, neuron_grad = lax.psum((gate_part, up_part, neuron_part), ("feature", "dp"))
+    spots_place = lambda local_block, link_axis, which_axis: lax.psum(
+        lax.psum(local_block, link_axis), which_axis
+    )
+    gate_pre, up_pre, neuron_grad = spots_place((gate_part, up_part, neuron_part), "dp", "feature")
     gate_factor, up_factor = factors(gate_pre, up_pre)
     per_block = math.gcd(features, 8)
     grouped_rows = neuron_grad.reshape(features // per_block, per_block, ffblk)

time: 1140 us -> 1010 us (0.89)
  waiting for transfers between devices: 968 us -> 839 us
    psum x1 -> x2, waiting for transfers between devices: 283 us -> 154 us  [the longest x1 80.2 us: on_device(): lax.psum(lax.psum(local_block, link_axis), which_axis)]
    unnamed x4 -> x5, waiting for transfers between devices: 487 us -> 487 us
  transfers between devices with their start and end apart: 3 -> 4, of which waited for: 3 -> 4; matrix products, arithmetic and copies ran while one was open for 1% -> 1% of each run, Pallas kernels for 0% -> 0%
where the time goes in v1:
time: 1010 us
  waiting for transfers between devices  839 us (83%)
  blocking collectives  99.8 us (10%)
  local copies, waits for them, and re-layouts  33.6 us (3%)
  matrix products  15.8 us (2%)
  between operations  13.2 us (1%)
    unnamed x5, waiting for transfers between devices  487 us
    psum x1, waiting for transfers between devices, on_device(): width_full = lax.psum(width_part, 'tensor')  199 us
    psum x1, blocking collectives, on_device(): lax.psum(jnp.dot(picker, down_encoder, preferred_element_type=jnp.float32...  99.8 us
    psum x1, waiting for transfers between devices, on_device(): lax.psum(lax.psum(local_block, link_axis), which_axis)  80.2 us
    psum x1, waiting for transfers between devices, on_device(): lax.psum(local_block, link_axis)  73.8 us
  transfers between devices with their start and end apart: 4, of which 4 were waited for; matrix products, arithmetic and copies ran while one was open for 1% of the time, Pallas kernels for 0%

profile of v1, /device:TPU:2, one launch (start us, length us, event | category | flops | bytes accessed | tf_op | source)
XLA Modules:
  0.0 1008.5 jit_solution(2070131700483383995)
XLA Ops:
  6.6 0.8 broadcast_subtract_fusion
  7.4 1.6 fusion.5
  9.0 99.8 %psum.56 = bf16[32,128]{1,0:T(8,128)(2,1)S(1)} all-reduce(f32[32,128]{1,0:T(8,128)S(1)} %fusion.5), channel_id=1, replica_groups=mesh['tensor'=16,'feature'=8,'dp'=4] {'tensor'}, use_global_device_ids=true, to_apply=%region_0.0 | all-reduce | flops 4096 | bytes 24576 | tf_op jit(solution)/shard_map/psum | solution.py:61
  108.8 2.0 fusion.13
  110.8 1.7 fusion.14
  112.5 1.0 fusion.15
  113.5 73.8 %all-reduce.14.cloned.1.call-done = (f32[32,1792]{1,0:T(8,128)}, f32[64,1792]{1,0:T(8,128)}, f32[64,1792]{1,0:T(8,128)}) async-done(((f32[32,1792]{1,0:T(8,128)}, f32[64,1792]{1,0:T(8,128)}, f32[64,1792]{1,0:T(8,128)}), (f32[32,1792]{1,0:T(8,128)}, f32[64,1792]{1,0:T(8,128)}, f32[64,1792]{1,0:T(8,128)})) %all-reduce.14.cloned.1.call-update) | async-done | bytes 1146896 | tf_op jit(solution)/shard_map/psum | solution.py:69
  187.5 80.2 %all-reduce.12.cloned.1.call-done = (f32[4,8,1792]{2,1,0:T(8,128)}, f32[64,1792]{1,0:T(8,128)}, f32[64,1792]{1,0:T(8,128)}) async-done(((f32[4,8,1792]{2,1,0:T(8,128)}, f32[64,1792]{1,0:T(8,128)}, f32[64,1792]{1,0:T(8,128)}), (f32[4,8,1792]{2,1,0:T(8,128)}, f32[64,1792]{1,0:T(8,128)}, f32[64,1792]{1,0:T(8,128)})) %all-reduce.12.cloned.1.call-update) | async-done | bytes 1146896 | tf_op jit(solution)/shard_map/psum | solution.py:68
  267.7 1.4 fusion.6
  269.1 16.5 %while.10 = (s32[]{:T(128)}, f32[4,8,64,128]{3,1,0,2:T(8,128)}, f32[4,8,1792]{2,1,0:T(8,128)}, f32[64,1792]{1,0:T(8,128)S(1)}, bf16[128,1792]{1,0:T(8,128)(2,1)S...) while((s32[]{:T(128)}, f32[4,8,64,128]{3,1,0,2:T(8,128)}, f32[4,8,1792]{2,1,0:T(8,128)}, ...), condition=%wide.region_8.9_spmd, body=%wide.region_7.8_spmd.sunk | while | flops 473497600 | bytes 12493429 | solution.py:95
  269.1 0.8 dynamic-slice_bitcast_fusion.3
  269.9 0.7 multiply_convert_fusion.3
  272.3 0.9 copy_dynamic-update-slice_fusion.2
  273.2 0.8 dynamic-slice_bitcast_fusion.3
  274.0 0.7 multiply_convert_fusion.3
  275.8 0.6 convolution_add_fusion.2
  276.4 0.9 copy_dynamic-update-slice_fusion.2
  277.3 0.8 dynamic-slice_bitcast_fusion.3
  278.1 0.7 multiply_convert_fusion.3
  280.5 0.9 copy_dynamic-update-slice_fusion.2
  281.4 0.8 dynamic-slice_bitcast_fusion.3
  282.3 0.7 multiply_convert_fusion.3
  284.7 0.9 copy_dynamic-update-slice_fusion.2
  285.8 12.1 %gather_fusion = bf16[4096,128]{1,0:T(8,128)(2,1)S(1)} fusion(bf16[8192,128]{1,0:T(8,128)(2,1)S(1)} %copy-done, s32[4096]{0:T(1024)S(1)} %broadcast_clamp_fusion), kind=kCustom, calls=%fused_computation | custom fusion | bytes 2113536 | tf_op jit(solution)/shard_map/jit(_take)/gather | solution.py:99
  297.9 198.5 %all-reduce.8.cloned.1.call-done = f32[32,64,128]{2,0,1:T(8,128)} async-done(((f32[32,64,128]{2,0,1:T(8,128)}), f32[32,64,128]{2,0,1:T(8,128)}) %all-reduce.8.cloned.1.call-update) | async-done | bytes 1048592 | tf_op jit(solution)/shard_map/psum | solution.py:101
  496.4 4.4 convolution_bitcast_fusion
  500.8 1.8 copy.18
  502.6 3.2 reshape.39
  505.8 3.4 copy.19
  509.1 4.7 copy.20
  513.8 486.8 %all-reduce.10.cloned.1.call-done = f32[512,4,16,4]{2,3,1,0:T(4,128)} async-done(((f32[512,4,16,4]{2,3,1,0:T(4,128)}), f32[512,4,16,4]{2,3,1,0:T(4,128)}) %all-reduce.10.cloned.1.call-update) | async-done | bytes 524304
  1000.7 1.3 fusion.8
  (37 shorter events, 6.3 us)
Async XLA Ops:
  6.5 279.2 %copy-start = (bf16[8192,128]{1,0:T(8,128)(2,1)S(1)}, bf16[8192,128]{1,0:T(8,128)(2,1)}, u32[]{:S(2)}) copy-start(bf16[8192,128]{1,0:T(8,128)(2,1)} %param.17) | copy-start | bytes 6291460
  6.5 104.3 %copy-start.1 = (bf16[128,1792]{1,0:T(8,128)(2,1)S(1)}, bf16[128,1792]{1,0:T(8,128)(2,1)}, u32[]{:S(2)}) copy-start(bf16[128,1792]{1,0:T(8,128)(2,1)} %param.12) | copy-start | bytes 1376260
  6.5 105.9 %copy-start.3 = (bf16[1792,128]{1,0:T(8,128)(2,1)S(1)}, bf16[1792,128]{1,0:T(8,128)(2,1)}, u32[]{:S(2)}) copy-start(bf16[1792,128]{1,0:T(8,128)(2,1)} %param.14) | copy-start | bytes 1376260
  6.5 180.8 %all-reduce.14.cloned.1.call-start = ((), (), s32[]{:S(2)}) async-start(), calls=%async_computation.3 | async-start | bytes 2293760 | tf_op jit(solution)/shard_map/psum | solution.py:69
  113.5 154.2 %all-reduce.12.cloned.1.call-start = ((), (), s32[]{:S(2)}) async-start(), calls=%async_computation.2 | async-start | bytes 2293760 | tf_op jit(solution)/shard_map/psum | solution.py:68
  187.4 309.0 %all-reduce.8.cloned.1.call-start = ((), (), s32[]{:S(2)}) async-start(), calls=%async_computation | async-start | bytes 2097152 | tf_op jit(solution)/shard_map/psum | solution.py:101
  269.0 16.6 %copy-start.4 = (s32[64,64]{1,0:T(8,128)S(1)}, s32[64,64]{1,0:T(8,128)}, u32[]{:S(2)}) copy-start(s32[64,64]{1,0:T(8,128)} %param.18) | copy-start | bytes 49156
  270.6 1.0 copy-start.2
  274.7 1.0 copy-start.2
  278.8 1.0 copy-start.2
  283.0 1.0 copy-start.2
  285.6 715.1 %all-reduce.10.cloned.1.call-start = ((), (), s32[]{:S(2)}) async-start(), calls=%async_computation.1 | async-start | bytes 8388608
  513.8 486.8 %copy-start.5 = (f32[16,4]{0,1:T(4,128)S(1)}, f32[16,4]{0,1:T(4,128)}, u32[]{:S(2)}) copy-start(f32[16,4]{0,1:T(4,128)} %param.19) | copy-start | bytes 772
Sparse Core Ops, SparseCore 0:
  113.6 73.7 all-reduce.13
  189.9 77.6 all-reduce.11
  285.7 210.6 all-reduce.7
  514.0 486.6 all-reduce.9

commit v2 on v0

--- a/solution.py
+++ b/solution.py
@@ -3,6 +3,11 @@
 import jax.numpy as jnp
 from jax import lax
 from jax.sharding import PartitionSpec as P
+
+
+def summed_here(x, mesh_axis):
+    shards = lax.all_gather(x, mesh_axis)
+    return jnp.sum(shards, axis=0)
 
 
 def factors(gate_pre, up_pre):
@@ -95,7 +100,7 @@
     owner_mask = jnp.logical_and(local_latents >= 0, local_latents < dec_rows)
     picked = jnp.take(up_decoder, jnp.clip(local_latents, 0, dec_rows - 1), axis=0)
     picked = picked * owner_mask[:, :, None].astype(jnp.bfloat16)
-    width_full = lax.psum(width_part, "tensor")
+    width_full = summed_here(width_part, "tensor")
     partial_value = jnp.einsum(
         "ftd,tkd->ftk", width_full, picked.astype(jnp.float32), precision=lax.Precision.HIGHEST
     )

time: 1140 us -> 1320 us (1.16)
  waiting for transfers between devices: 968 us -> 1140 us
    all_gather x0 -> x1, waiting for transfers between devices: none -> 371 us  [summed_here(): shards = lax.all_gather(x, mesh_axis)]
    psum x1 -> x0, waiting for transfers between devices: 198 us -> none  [on_device(): width_full = lax.psum(width_part, 'tensor')]
where the time goes in v2:
time: 1320 us
  waiting for transfers between devices  1140 us (86%)
  blocking collectives  99.8 us (8%)
  local copies, waits for them, and re-layouts  32.9 us (2%)
  matrix products  15.8 us (1%)
  other arithmetic  15.1 us (1%)
    unnamed x4, waiting for transfers between devices  490 us
    all_gather x1, waiting for transfers between devices, summed_here(): shards = lax.all_gather(x, mesh_axis)  371 us
    psum x1, waiting for transfers between devices, on_device(): lax.psum((gate_part, up_part, neuron_part), ('feature', 'dp'))  283 us
    psum x1, blocking collectives, on_device(): lax.psum(jnp.dot(picker, down_encoder, preferred_element_type=jnp.float32...  99.8 us
  transfers between devices with their start and end apart: 3, of which 3 were waited for; matrix products, arithmetic and copies ran while one was open for 1% of the time, Pallas kernels for 0%

profile of v2, /device:TPU:2, one launch (start us, length us, event | category | flops | bytes accessed | tf_op | source)
XLA Modules:
  0.0 1321.5 jit_solution(11272286426567000991)
XLA Ops:
  6.6 0.8 broadcast_subtract_fusion
  7.4 1.6 fusion.6
  9.0 99.8 %psum.28 = bf16[32,128]{1,0:T(8,128)(2,1)S(1)} all-reduce(f32[32,128]{1,0:T(8,128)S(1)} %fusion.6), channel_id=1, replica_groups=mesh['tensor'=16,'feature'=8,'dp'=4] {'tensor'}, use_global_device_ids=true, to_apply=%region_0.0 | all-reduce | flops 4096 | bytes 24576 | tf_op jit(solution)/shard_map/psum | solution.py:66
  108.8 2.0 fusion.13
  110.8 1.7 fusion.14
  112.5 1.0 convolution_bitcast_fusion
  113.6 283.3 %all-reduce.7.cloned.1.call-done = (f32[4,8,1792]{2,1,0:T(8,128)}, f32[64,1792]{1,0:T(8,128)}, f32[64,1792]{1,0:T(8,128)}) async-done(((f32[4,8,1792]{2,1,0:T(8,128)}, f32[64,1792]{1,0:T(8,128)}, f32[64,1792]{1,0:T(8,128)}), (f32[4,8,1792]{2,1,0:T(8,128)}, f32[64,1792]{1,0:T(8,128)}, f32[64,1792]{1,0:T(8,128)})) %all-reduce.7.cloned.1.call-update) | async-done | bytes 1146896 | tf_op jit(solution)/shard_map/psum | solution.py:73
  396.8 1.4 fusion.7
  398.2 15.8 %while.10 = (s32[]{:T(128)}, f32[4,8,64,128]{3,2,1,0:T(8,128)}, f32[4,8,1792]{2,1,0:T(8,128)}, f32[64,1792]{1,0:T(8,128)S(1)}, bf16[128,1792]{1,0:T(8,128)(2,1)S...) while((s32[]{:T(128)}, f32[4,8,64,128]{3,2,1,0:T(8,128)}, f32[4,8,1792]{2,1,0:T(8,128)}, ...), condition=%wide.region_5.6_spmd, body=%wide.region_4.5_spmd.sunk | while | flops 473497600 | bytes 12493429 | solution.py:97
  398.2 0.8 dynamic-slice_bitcast_fusion.3
  399.0 0.7 multiply_convert_fusion.3
  400.8 0.6 convolution_add_fusion.2
  401.4 0.7 constant_dynamic-update-slice_fusion.2
  402.2 0.8 dynamic-slice_bitcast_fusion.3
  403.0 0.7 multiply_convert_fusion.3
  405.4 0.7 constant_dynamic-update-slice_fusion.2
  406.1 0.8 dynamic-slice_bitcast_fusion.3
  407.0 0.7 multiply_convert_fusion.3
  409.4 0.7 constant_dynamic-update-slice_fusion.2
  410.1 0.8 dynamic-slice_bitcast_fusion.3
  410.9 0.7 multiply_convert_fusion.3
  413.3 0.7 constant_dynamic-update-slice_fusion.2
  414.2 12.1 gather_fusion
  426.4 371.0 %all-gather.2.cloned.1.call-done = f32[16,32,64,128]{3,2,1,0:T(8,128)} async-done(((f32[1,32,64,128]{3,2,1,0:T(8,128)}), f32[16,32,64,128]{3,2,1,0:T(8,128)}) %all-gather.2.cloned.1.call-update) | async-done | bytes 16777232 | tf_op jit(solution)/shard_map/all_gather | solution.py:9
  797.4 8.7 reduce_sum.9
  806.1 4.4 convolution_bitcast_fusion.1
  810.5 1.8 copy.15
  812.3 3.2 reshape.35
  815.5 3.4 copy.16
  818.9 4.7 copy.17
  823.6 490.1 %all-reduce.5.cloned.1.call-done = f32[512,4,16,4]{2,3,1,0:T(4,128)} async-done(((f32[512,4,16,4]{2,3,1,0:T(4,128)}), f32[512,4,16,4]{2,3,1,0:T(4,128)}) %all-reduce.5.cloned.1.call-update) | async-done | bytes 524304
  1313.6 1.3 fusion.9
  (35 shorter events, 6.2 us)
Async XLA Ops:
  6.5 407.7 %copy-start = (bf16[8192,128]{1,0:T(8,128)(2,1)S(1)}, bf16[8192,128]{1,0:T(8,128)(2,1)}, u32[]{:S(2)}) copy-start(bf16[8192,128]{1,0:T(8,128)(2,1)} %param.17) | copy-start | bytes 6291460
  6.5 104.3 %copy-start.1 = (bf16[128,1792]{1,0:T(8,128)(2,1)S(1)}, bf16[128,1792]{1,0:T(8,128)(2,1)}, u32[]{:S(2)}) copy-start(bf16[128,1792]{1,0:T(8,128)(2,1)} %param.12) | copy-start | bytes 1376260
  6.5 106.0 %copy-start.3 = (bf16[1792,128]{1,0:T(8,128)(2,1)S(1)}, bf16[1792,128]{1,0:T(8,128)(2,1)}, u32[]{:S(2)}) copy-start(bf16[1792,128]{1,0:T(8,128)(2,1)} %param.14) | copy-start | bytes 1376260
  6.5 390.3 %all-reduce.7.cloned.1.call-start = ((), (), s32[]{:S(2)}) async-start(), calls=%async_computation.2 | async-start | bytes 2293760 | tf_op jit(solution)/shard_map/psum | solution.py:73
  113.5 683.9 %all-gather.2.cloned.1.call-start = ((), (), s32[]{:S(2)}) async-start(), calls=%async_computation | async-start | bytes 17825792 | tf_op jit(solution)/shard_map/all_gather | solution.py:9
  398.2 15.9 %copy-start.4 = (s32[64,64]{1,0:T(8,128)S(1)}, s32[64,64]{1,0:T(8,128)}, u32[]{:S(2)}) copy-start(s32[64,64]{1,0:T(8,128)} %param.18) | copy-start | bytes 49156
  399.8 1.0 copy-start.2
  403.7 1.0 copy-start.2
  407.7 1.0 copy-start.2
  411.6 1.0 copy-start.2
  414.1 899.6 %all-reduce.5.cloned.1.call-start = ((), (), s32[]{:S(2)}) async-start(), calls=%async_computation.1 | async-start | bytes 8388608
  823.5 490.1 %copy-start.5 = (f32[16,4]{0,1:T(4,128)S(1)}, f32[16,4]{0,1:T(4,128)}, u32[]{:S(2)}) copy-start(f32[16,4]{0,1:T(4,128)} %param.19) | copy-start | bytes 772
Sparse Core Ops, SparseCore 0:
  113.6 283.1 all-reduce.6
  414.2 383.1 all-gather.1
  823.7 489.9 all-reduce.4
